TPU v7x, 256 devices: a whole 4x4x8 slice. The times are simulated.
256 devices in a mesh: dp: 16 (over y, x), mem: 16 (over z, core).
Axes of the slice: x: 4, y: 4, z: 8, core: 2. Of those that a mesh axis runs over, the one named last changes fastest.
Arguments:
- tokens: bfloat16 [131072, 2048], P(('dp', 'mem')), may hold values from -320 to 320
- q_weight: bfloat16 [2048, 1024], replicated, may hold values from -0.13 to 0.13
- memory_keys: bfloat16 [16, 64, 128, 512], P('dp', 'mem'), may hold values from -45 to 45
- memory_values: bfloat16 [16, 64, 128, 512], P('dp', 'mem'), may hold values from -6 to 6
- retrieved_block_index: int32 [16, 16, 8], P('dp', 'mem'), may hold values from 0 to 63, as said below
- d_context: bfloat16 [131072, 1024], P(('dp', 'mem')), may hold values from -6 to 6
Outputs:
- context: bfloat16 [131072, 1024], P(('dp', 'mem'))
- grad_tokens: bfloat16 [131072, 2048], P(('dp', 'mem'))
- grad_q_weight: float32 [2048, 1024], P(('dp', 'mem'))
Inputs may be any that keep to these rules, and one draw needn't show every extreme that they name: `retrieved_block_index`: A segment's 8 ids are distinct; at most 2 of them lie in one memory shard (ids k * 4 to (k + 1) * 4 - 1), and in every segment exactly three shards hold 2 of them.
All inputs are finite; a program needn't handle non-finite values.
Results may differ from a plain program's by a relative error of at most 0.015.
Values may be sent and summed in bfloat16 or wider, within the bound.
A program may use at most 128 MiB of HBM per device.

v0:
```python
import jax
import jax.numpy as jnp
from jax import lax
from jax.sharding import PartitionSpec as P

KVH = 4
HD = 128
TOPB = 8
CAP = 2
GRP = 2


def on_device(tokens, q_weight, memory_keys, memory_values, retrieved_block_index, d_context):
    score_scale = 1.0 / HD**0.5
    memory_block_count = lax.axis_size("mem")
    blocks_here = memory_keys.shape[1]
    desired_blocks = retrieved_block_index[0, 0]
    seg_rows = tokens.shape[0]
    home_shard = desired_blocks // blocks_here
    resident_slot_index = desired_blocks % blocks_here
    earlier = jnp.arange(TOPB)[None, :] < jnp.arange(TOPB)[:, None]
    order_rank = jnp.sum(earlier & (home_shard[None, :] == home_shard[:, None]), axis=1)
    slot_ids = jnp.arange(CAP)
    matches = (home_shard[None, :, None] == jnp.arange(memory_block_count)[:, None, None]) & (
        order_rank[None, :, None] == slot_ids[None, None, :]
    )
    picked = jnp.sum(jnp.where(matches, resident_slot_index[None, :, None], 0), axis=1)
    wishes = jnp.where(jnp.any(matches, axis=1), picked, -1)
    requested = lax.all_to_all(wishes, "mem", split_axis=0, concat_axis=0, tiled=True)
    present = (requested >= 0)[:, :, None, None]
    safe_index = jnp.maximum(requested, 0)
    send_keys = jnp.where(present, memory_keys[0][safe_index], jnp.zeros((), jnp.bfloat16))
    send_values = jnp.where(present, memory_values[0][safe_index], jnp.zeros((), jnp.bfloat16))
    got_keys, got_values = (
        lax.all_to_all(send_keys, "mem", split_axis=0, concat_axis=0, tiled=True),
        lax.all_to_all(send_values, "mem", split_axis=0, concat_axis=0, tiled=True),
    )
    position = home_shard * CAP + order_rank
    keys = got_keys.reshape(-1, got_keys.shape[2], got_keys.shape[3])[position].reshape(-1, KVH, HD)
    values = got_values.reshape(-1, got_values.shape[2], got_values.shape[3])[position].reshape(
        -1, KVH, HD
    )
    queries = jnp.dot(tokens, q_weight, preferred_element_type=jnp.float32).astype(jnp.bfloat16)
    heads = queries.reshape(seg_rows, KVH, GRP, HD)
    scores = (
        jnp.einsum("skrd,tkd->krst", heads, keys, preferred_element_type=jnp.float32) * score_scale
    )
    top = jnp.max(scores, axis=-1, keepdims=True)
    expo = jnp.exp(scores - top)
    probs = expo / jnp.sum(expo, axis=-1, keepdims=True)
    probs_low = probs.astype(jnp.bfloat16)
    context = jnp.einsum("krst,tkd->skrd", probs_low, values, preferred_element_type=jnp.float32)
    context = context.reshape(seg_rows, -1).astype(jnp.bfloat16)
    d_out = d_context.reshape(seg_rows, KVH, GRP, HD)
    d_probs = jnp.einsum("skrd,tkd->krst", d_out, values, preferred_element_type=jnp.float32)
    row_delta = jnp.sum(probs * d_probs, axis=-1, keepdims=True)
    d_scores = (probs * (d_probs - row_delta) * score_scale).astype(jnp.bfloat16)
    d_query = jnp.einsum("krst,tkd->skrd", d_scores, keys, preferred_element_type=jnp.float32)
    d_query = d_query.reshape(seg_rows, -1).astype(jnp.bfloat16)
    weight_grad = lax.psum_scatter(
        lax.dot_general(
            tokens, d_query, (((0,), (0,)), ((), ())), preferred_element_type=jnp.float32
        ),
        ("dp", "mem"),
        scatter_dimension=0,
        tiled=True,
    )
    grad_tokens = lax.dot_general(
        d_query, q_weight, (((1,), (1,)), ((), ())), preferred_element_type=jnp.float32
    ).astype(jnp.bfloat16)
    return (context, grad_tokens, weight_grad)


def solution(mesh):
    return jax.shard_map(
        on_device,
        mesh=mesh,
        in_specs=(
            P(("dp", "mem"), None),
            P(),
            P("dp", "mem", None, None),
            P("dp", "mem", None, None),
            P("dp", "mem", None),
            P(("dp", "mem"), None),
        ),
        out_specs=(P(("dp", "mem"), None), P(("dp", "mem"), None), P(("dp", "mem"), None)),
        check_vma=False,
    )
```

profile of v0, /device:TPU:1, one launch (start us, length us, event | category | flops | bytes accessed | tf_op | source)
XLA Modules:
  0.0 1583.9 jit_solution(14278011281710197330)
XLA Ops:
  7.2 0.0 copy-start
  7.2 0.8 and_select_fusion.2
  8.0 0.2 convert_reduce_fusion
  8.2 0.1 iota_compare_fusion.1
  8.3 0.1 and_reduce_fusion
  8.4 0.1 fusion.32
  8.4 0.1 copy.55
  8.5 16.8 %all_to_all.16 = s32[16,1,2]{2,1,0:T(1,128)S(1)} all-to-all(s32[16,1,2]{2,1,0:T(1,128)S(1)} %copy.55), channel_id=1, replica_groups=mesh['dp'=16,'mem'=16] {'mem'}, dimensions={0} | all-to-all | bytes 256 | tf_op jit(solution)/shard_map/all_to_all | solution.py:29
  25.4 0.1 reshape.293
  25.5 0.0 copy-start.1
  25.5 3.9 gather_fusion.2
  29.3 0.0 copy-done.1
  29.4 2.8 gather_fusion
  32.2 0.1 copy.56
  32.3 0.1 copy.57
  32.4 5.1 broadcast_select_fusion
  37.5 99.8 %all_to_all.17 = bf16[16,2,128,512]{3,2,1,0:T(8,128)(2,1)} all-to-all(bf16[16,2,128,512]{3,2,1,0:T(8,128)(2,1)S(1)} %get-tuple-element.18), channel_id=1, replica_groups=mesh['dp'=16,'mem'=16] {'mem'}, dimensions={0} | all-to-all | bytes 8388608 | tf_op jit(solution)/shard_map/all_to_all | solution.py:35
  137.3 4.4 all-to-all-start.1
  141.8 0.0 copy-start.2
  141.8 0.0 reduce-scatter.4.cloned.1.call-start
  141.8 0.0 copy-done
  141.8 5.6 convolution_convert_fusion.1
  147.4 0.0 copy-start.3
  147.4 2.6 reshape.289
  150.0 0.0 copy-done.2
  150.0 1.5 reshape.290
  151.5 0.0 copy-done.3
  151.6 2.8 gather_fusion.3
  154.4 1.1 reshape.288
  155.5 2.4 copy.72
  157.9 76.1 %all-to-all-done.1 = bf16[16,2,128,512]{3,2,1,0:T(8,128)(2,1)} async-done(((bf16[16,2,128,512]{3,2,1,0:T(8,128)(2,1)}), bf16[16,2,128,512]{3,2,1,0:T(8,128)(2,1)}, u32[]{:S(2)}, u32[]{:S(2)}) %all-to-all-start.1) | async-done | bytes 4194336 | tf_op jit(solution)/shard_map/all_to_all | solution.py:36
  234.0 3.8 gather_fusion.1
  237.8 1.3 reshape.331
  239.1 12.9 fusion.38
  252.0 9.3 fusion.22
  261.3 23.2 %fusion.17 = bf16[4,128,2,512]{3,1,2,0:T(8,128)(2,1)} fusion(bf16[1024,4,128,1]{0,2,3,1:T(8,128)(2,1)} %copy.72, f32[4,1024,512,2]{2,1,3,0:T(8,128)} %fusion.22, f32[4,2,512,1024]{2,3,1,0:T(8,128)} %get-tuple-element.23, f32[4,2,512]{2,1,0:T(2,128)S(1)} %get-tuple-element.22), kind=kOutput, calls=%fused_computation.27 | convolution fusion | flops 1103631360 | bytes 35667968 | tf_op jit(solution)/shard_map/krst,tkd->skrd/dot_general | solution.py:58
  284.5 6.8 convolution_bitcast_fusion
  291.3 9.3 copy.82
  300.6 0.0 reduce-scatter.4.cloned.1.call-update
  300.6 1.5 copy.74
  302.1 7.4 fusion.18
  309.5 1.3 copy.66
  310.8 6.2 convolution_convert_fusion
  317.0 1260.1 %reduce-scatter.4.cloned.1.call-done = f32[8,1024]{1,0:T(8,128)} async-done(((f32[2048,1024]{1,0:T(8,128)}), f32[8,1024]{1,0:T(8,128)}) %reduce-scatter.4.cloned.1.call-update) | async-done | bytes 32784
  (7 shorter events, 0.1 us)
Async XLA Ops:
  7.2 134.7 %copy-start = (bf16[512,2048]{1,0:T(8,128)(2,1)S(1)}, bf16[512,2048]{1,0:T(8,128)(2,1)}, u32[]{:S(2)}) copy-start(bf16[512,2048]{1,0:T(8,128)(2,1)} %param.6) | copy-start | bytes 6291460
  25.5 3.9 copy-start.1
  137.3 96.7 %all-to-all-start.1 = ((bf16[16,2,128,512]{3,2,1,0:T(8,128)(2,1)}), bf16[16,2,128,512]{3,2,1,0:T(8,128)(2,1)}, u32[]{:S(2)}, u32[]{:S(2)}) async-start(bf16[16,2,128,512]{3,2,1,0:T(8,128)(2,1)} %get-tuple-element.19), calls=%async_computation.1 | async-start | bytes 8388608 | tf_op jit(solution)/shard_map/all_to_all | solution.py:36
  141.8 8.2 copy-start.2
  141.8 1435.3 %reduce-scatter.4.cloned.1.call-start = ((), (), s32[]{:S(2)}) async-start(), calls=%async_computation.4 | async-start | bytes 8421376
  147.4 4.1 copy-start.3
Sparse Core Ops, SparseCore 0:
  300.7 1276.3 reduce-scatter.3
where the time goes:
time: 1590 us; the launch traced here: 1580 us
  waiting for transfers between devices  1340 us (84%)
  blocking collectives  117 us (7%)
  matrix products  71.4 us (4%)
  local copies, waits for them, and re-layouts  34.7 us (2%)
    unnamed x2, waiting for transfers between devices  1260 us
    all_to_all x1, blocking collectives, on_device(): lax.all_to_all(send_keys, 'mem', split_axis=0, concat_axis=0, tiled=True)  99.8 us
    all_to_all x1, waiting for transfers between devices, on_device(): lax.all_to_all(send_values, 'mem', split_axis=0, concat_axis=0, tiled=True)  76.1 us
  transfers between devices with their start and end apart: 2, of which 2 were waited for; matrix products, arithmetic and copies ran while one was open for 2% of the time, Pallas kernels for 0%

commit v1 on v0

v1 whole, which is shorter than its diff:
```python
import math

import jax
import jax.numpy as jnp
from jax import lax
from jax.experimental import pallas as pl
from jax.experimental.pallas import tpu as pltpu
from jax.sharding import PartitionSpec as P

KVH = 4
HD = 128
TOPB = 8
SEG = 512
D = 2048
QW = 1024
NZ = 8
NMEM = 16
NDP = 16
BLK = 4
ROWS = 256
SCALE = 1.0 / HD**0.5
EXP2_SCALE = SCALE * math.log2(math.e)
MESH = pl.DeviceIdType.MESH
F32 = jnp.float32
BF16 = jnp.bfloat16


def dot(a, b):
    return jnp.dot(a, b, preferred_element_type=F32)


def kernel(
    tok_hbm, qw_hbm, mk_hbm, mv_hbm, idx, dctx_hbm,
    ctx_hbm, gt_hbm, gw_hbm,
    kv0, kv1, kv2, kv3, tok, qw, dctx, tok_t, qw_t, q, ctx, dq, gt,
    k_sel, k_t, v_one, v_t,
    g_keep, g_send, g_recv, g_sum, dp_recv,
    za_send, za_recv, zb_send, zb_recv, gw,
    in_sem, own_sem, ring_send, ring_recv, sib_send, sib_recv,
    pair_send, pair_recv, dp_send, dp_rsem, z_send, z_rsem, out_sem,
):
    kv = (kv0, kv1, kv2, kv3)
    dp = lax.axis_index("dp")
    mem = lax.axis_index("mem")
    z = lax.div(mem, 2)
    core = lax.rem(mem, 2)

    def at_z(step):
        return lax.rem(z + step + NZ, NZ) * 2 + core

    def dev(m):
        return (dp, m)

    sib = dev(z * 2 + 1 - core)

    def shard(m):
        return pl.ds(pl.multiple_of(m * BLK, BLK), BLK)

    loads = [
        pltpu.make_async_copy(tok_hbm, tok, in_sem.at[0]),
        pltpu.make_async_copy(qw_hbm, qw, in_sem.at[1]),
        pltpu.make_async_copy(dctx_hbm, dctx, in_sem.at[2]),
    ]
    own = [
        [
            pltpu.make_async_copy(
                src.at[0, :, :, pl.ds(h * HD, HD)], kv[h].at[t, shard(mem)], own_sem.at[h, t]
            )
            for t, src in enumerate((mk_hbm, mv_hbm))
        ]
        for h in range(KVH)
    ]
    for h in range(KVH):
        for c in own[h]:
            c.start()
    for c in loads:
        c.start()

    barrier = pltpu.get_barrier_semaphore()

    def greet(j, carry):
        pl.semaphore_signal(
            barrier, inc=1, device_id=dev(lax.rem(mem + j, NMEM)), device_id_type=MESH
        )
        pl.semaphore_signal(
            barrier, inc=1, device_id=(lax.rem(dp + j, NDP), mem), device_id_type=MESH
        )
        return carry

    lax.fori_loop(1, NMEM, greet, 0)
    pl.semaphore_wait(barrier, 2 * (NMEM - 1))

    def ring(h, t, way, step):
        sign = 1 if way == 0 else -1
        piece = kv[h].at[t, shard(at_z(-sign * (step - 1)))]
        return pltpu.make_async_remote_copy(
            src_ref=piece, dst_ref=piece,
            send_sem=ring_send.at[h, t], recv_sem=ring_recv.at[h, t, way, step - 1],
            device_id=dev(at_z(sign)), device_id_type=MESH,
        )

    def ring_arrival(h, t, way, step):
        sign = 1 if way == 0 else -1
        piece = kv[h].at[t, shard(at_z(-sign * step))]
        pltpu.make_async_remote_copy(
            src_ref=piece, dst_ref=piece,
            send_sem=ring_send.at[h, t], recv_sem=ring_recv.at[h, t, way, step - 1],
            device_id=dev(at_z(sign)), device_id_type=MESH,
        ).wait_recv()

    def to_sib(h, m):
        piece = kv[h].at[:, shard(m)]
        pltpu.make_async_remote_copy(
            src_ref=piece, dst_ref=piece, send_sem=sib_send.at[h], recv_sem=sib_recv.at[h],
            device_id=sib, device_id_type=MESH,
        ).start()

    def sib_all(h):
        half = kv[h].at[:, pl.ds(0, NZ * BLK)]
        return pltpu.make_async_remote_copy(
            src_ref=half, dst_ref=half, send_sem=sib_send.at[h], recv_sem=sib_recv.at[h],
            device_id=sib, device_id_type=MESH,
        )

    def send_own(h):
        for t in range(2):
            own[h][t].wait()
            for way in range(2):
                ring(h, t, way, 1).start()
        to_sib(h, mem)

    def ring_step(h, t, step):
        for way in range(2):
            if step < 4 or t == way:
                ring_arrival(h, t, way, step)
                if step < 3 or (step == 3 and t == way):
                    ring(h, t, way, step + 1).start()

    def pass_to_sib(h, step):
        to_sib(h, at_z(-step))
        if step < 4:
            to_sib(h, at_z(step))

    def gather(h):
        for j in range(TOPB):
            b = idx[0, 0, j]
            rows = pl.ds(j * 128, 128)
            kb = kv[h][0, b]
            vb = kv[h][1, b]
            k_sel[rows, :] = kb
            k_t[:, rows] = kb.T
            v_one[rows, pl.ds(0, HD)] = vb
            v_t[:, rows] = vb.T

    def attend(h, first, r):
        j = 1 - core if first else core
        rows = pl.ds(r * ROWS, ROWS)
        sub = pl.ds(pl.multiple_of(j * HD, HD), HD)
        full = pl.ds(pl.multiple_of((2 * h + j) * HD, HD), HD)
        do = dctx[rows, full]
        s = dot(q[h, rows, sub], k_t[...])
        top = jnp.max(s, axis=-1, keepdims=True)
        e = jnp.exp2((s - top) * EXP2_SCALE)
        pv = dot(e.astype(BF16), v_one[...])
        inv = 1.0 / pv[:, HD:]
        c = pv[:, :HD] * inv
        ctx[rows, full] = c.astype(BF16)
        d_p = dot(do, v_t[...])
        delta = jnp.sum(do.astype(F32) * c, axis=-1, keepdims=True)
        ds = (e * (d_p - delta)).astype(BF16)
        dq[h, rows, sub] = (dot(ds, k_sel[...]) * (inv * SCALE)).astype(BF16)

    def weight_grad(h):
        def tile(i, carry):
            rows = pl.ds(pl.multiple_of(i * 256, 256), 256)
            g = dot(tok_t[rows, :], dq[h])
            lo, hi = g[:, :HD], g[:, HD:]
            g_keep[rows, :] = jnp.where(core == 0, lo, hi)
            g_send[h, rows, :] = jnp.where(core == 0, hi, lo).astype(BF16)
            return carry

        lax.fori_loop(0, D // 256, tile, 0)
        pair(h).start()

    def pair(h):
        return pltpu.make_async_remote_copy(
            src_ref=g_send.at[h], dst_ref=g_recv.at[h], send_sem=pair_send.at[h],
            recv_sem=pair_recv.at[h], device_id=sib, device_id_type=MESH,
        )

    def dp_start(h):
        pair(h).wait_recv()

        def tile(i, carry):
            rows = pl.ds(pl.multiple_of(i * 256, 256), 256)
            g_sum[h, rows, :] = (g_keep[rows, :] + g_recv[h, rows, :].astype(F32)).astype(BF16)
            return carry

        lax.fori_loop(0, D // 256, tile, 0)

        def send(j, carry):
            d = lax.rem(dp + j, NDP)
            pltpu.make_async_remote_copy(
                src_ref=g_sum.at[h, pl.ds(pl.multiple_of(d * 128, 128), 128)],
                dst_ref=dp_recv.at[h, j - 1], send_sem=dp_send.at[h], recv_sem=dp_rsem.at[h],
                device_id=(d, mem), device_id_type=MESH,
            ).start()
            return carry

        lax.fori_loop(1, NDP, send, 0)

    def dp_all(h):
        return pltpu.make_async_remote_copy(
            src_ref=dp_recv.at[h], dst_ref=dp_recv.at[h], send_sem=dp_send.at[h],
            recv_sem=dp_rsem.at[h], device_id=sib, device_id_type=MESH,
        )

    def dp_finish(h):
        dp_all(h).wait_recv()
        acc = g_sum[h, pl.ds(pl.multiple_of(dp * 128, 128), 128), :].astype(F32)
        for j in range(NDP - 1):
            acc = acc + dp_recv[h, j].astype(F32)
        acc = acc.reshape(NMEM, 8, HD)
        if h < KVH - 1:
            za_send[:, :, pl.ds(h * HD, HD)] = acc
        else:
            zb_send[...] = acc

    def z_start(n, src, dst):
        def send(j, carry):
            m = lax.rem(mem + j, NMEM)
            pltpu.make_async_remote_copy(
                src_ref=src.at[m], dst_ref=dst.at[j - 1], send_sem=z_send.at[n],
                recv_sem=z_rsem.at[n], device_id=dev(m), device_id_type=MESH,
            ).start()
            return carry

        lax.fori_loop(1, NMEM, send, 0)

    def z_all(n, dst):
        return pltpu.make_async_remote_copy(
            src_ref=dst, dst_ref=dst, send_sem=z_send.at[n], recv_sem=z_rsem.at[n],
            device_id=sib, device_id_type=MESH,
        )

    def z_finish(n, src, dst, heads):
        z_all(n, dst).wait_recv()
        same = src[mem]
        other = dst[0]
        for j in range(2, NMEM):
            if j % 2 == 0:
                same = same + dst[j - 1]
            else:
                other = other + dst[j - 1]
        for i, h in enumerate(heads):
            part = slice(i * HD, (i + 1) * HD)
            gw[:, pl.ds(pl.multiple_of(h * 256 + core * HD, HD), HD)] = same[:, part]
            gw[:, pl.ds(pl.multiple_of(h * 256 + (1 - core) * HD, HD), HD)] = other[:, part]

    v_one[:, pl.ds(HD, HD)] = jnp.ones((TOPB * 128, HD), BF16)

    send_own(0)
    send_own(1)

    def project(n):
        if n == 0:
            loads[0].wait()
            loads[1].wait()
        q[n] = dot(tok[...], qw[:, pl.ds(n * 256, 256)]).astype(BF16)

    def transposes(n):
        tok_t[pl.ds(n * 512, 512), :] = tok[:, pl.ds(n * 512, 512)].T
        qw_t[:, pl.ds(n * 512, 512)] = qw[pl.ds(n * 512, 512), :].T

    for h in range(KVH):
        for step in range(1, 5):
            ring_step(h, 0, step)
            if h == 0:
                project(step - 1)
            elif step == 2 and h >= 2:
                dp_start(h - 2)
            elif step == 3 and h == 1:
                pass
            ring_step(h, 1, step)
            pass_to_sib(h, step)
            if step == 2 and 1 <= h < KVH - 1:
                send_own(h + 1)
            if h == 0:
                transposes(step - 1)
                if step == 4:
                    loads[2].wait()
            else:
                attend(h - 1, step <= 2, (step - 1) % 2)
        if h >= 2:
            dp_finish(h - 2)
        sib_all(h).wait_recv()
        if h >= 1:
            weight_grad(h - 1)
        gather(h)

    dp_start(2)
    for step in range(4):
        attend(3, step < 2, step % 2)
    weight_grad(3)
    dp_finish(2)
    z_start(0, za_send, za_recv)
    ctx_out = pltpu.make_async_copy(ctx, ctx_hbm, out_sem.at[0])
    ctx_out.start()
    dp_start(3)

    def tokens_tile(n, carry):
        cols = pl.ds(pl.multiple_of(n * 512, 512), 512)
        acc = dot(dq[0], qw_t[pl.ds(0, 256), cols])
        for h in range(1, KVH):
            acc = acc + dot(dq[h], qw_t[pl.ds(h * 256, 256), cols])
        gt[:, cols] = acc.astype(BF16)
        return carry

    lax.fori_loop(0, D // 512, tokens_tile, 0)
    gt_out = pltpu.make_async_copy(gt, gt_hbm, out_sem.at[1])
    gt_out.start()
    z_finish(0, za_send, za_recv, (0, 1, 2))
    dp_finish(3)
    z_start(1, zb_send, zb_recv)
    z_finish(1, zb_send, zb_recv, (3,))
    gw_out = pltpu.make_async_copy(gw, gw_hbm, out_sem.at[2])
    gw_out.start()

    for h in range(KVH):
        for t in range(2):
            sent = kv[h].at[t, pl.ds(0, 7 * BLK)]
            pltpu.make_async_remote_copy(
                src_ref=sent, dst_ref=sent, send_sem=ring_send.at[h, t],
                recv_sem=ring_recv.at[h, t, 0, 0], device_id=sib, device_id_type=MESH,
            ).wait_send()
        sib_all(h).wait_send()
        pair(h).wait_send()
        dp_all(h).wait_send()
    z_all(0, za_recv).wait_send()
    z_all(1, zb_recv).wait_send()
    ctx_out.wait()
    gt_out.wait()
    gw_out.wait()


def on_device(tokens, q_weight, memory_keys, memory_values, retrieved_block_index, d_context):
    hbm = pl.BlockSpec(memory_space=pl.ANY)
    vmem = pltpu.VMEM
    dma = pltpu.SemaphoreType.DMA
    kv = vmem((2, NMEM * BLK, 128, HD), BF16)
    return pl.pallas_call(
        kernel,
        out_shape=(
            jax.ShapeDtypeStruct((SEG, QW), BF16),
            jax.ShapeDtypeStruct((SEG, D), BF16),
            jax.ShapeDtypeStruct((D // (NDP * NMEM), QW), F32),
        ),
        in_specs=[hbm, hbm, hbm, hbm, pl.BlockSpec(memory_space=pltpu.SMEM), hbm],
        out_specs=(hbm, hbm, hbm),
        scratch_shapes=[
            kv, kv, kv, kv,
            vmem((SEG, D), BF16),
            vmem((D, QW), BF16),
            vmem((SEG, QW), BF16),
            vmem((D, SEG), BF16),
            vmem((QW, D), BF16),
            vmem((KVH, SEG, 256), BF16),
            vmem((SEG, QW), BF16),
            vmem((KVH, SEG, 256), BF16),
            vmem((SEG, D), BF16),
            vmem((TOPB * 128, HD), BF16),
            vmem((HD, TOPB * 128), BF16),
            vmem((TOPB * 128, 2 * HD), BF16),
            vmem((HD, TOPB * 128), BF16),
            vmem((D, HD), F32),
            vmem((KVH, D, HD), BF16),
            vmem((KVH, D, HD), BF16),
            vmem((KVH, D, HD), BF16),
            vmem((KVH, NDP - 1, 128, HD), BF16),
            vmem((NMEM, 8, 3 * HD), F32),
            vmem((NMEM - 1, 8, 3 * HD), F32),
            vmem((NMEM, 8, HD), F32),
            vmem((NMEM - 1, 8, HD), F32),
            vmem((8, QW), F32),
            dma((3,)),
            dma((KVH, 2)),
            dma((KVH, 2)),
            dma((KVH, 2, 2, 4)),
            dma((KVH,)),
            dma((KVH,)),
            dma((KVH,)),
            dma((KVH,)),
            dma((KVH,)),
            dma((KVH,)),
            dma((2,)),
            dma((2,)),
            dma((3,)),
        ],
        compiler_params=pltpu.CompilerParams(
            collective_id=0, has_side_effects=True, vmem_limit_bytes=60 * 1024 * 1024
        ),
    )(tokens, q_weight, memory_keys, memory_values, retrieved_block_index, d_context)


def solution(mesh):
    return jax.shard_map(
        on_device,
        mesh=mesh,
        in_specs=(
            P(("dp", "mem"), None),
            P(),
            P("dp", "mem", None, None),
            P("dp", "mem", None, None),
            P("dp", "mem", None),
            P(("dp", "mem"), None),
        ),
        out_specs=(P(("dp", "mem"), None), P(("dp", "mem"), None), P(("dp", "mem"), None)),
        check_vma=False,
    )
```

time: 1590 us -> 146 us (0.09)
  waiting for transfers between devices: 1340 us -> 0 us
  Pallas kernels: 0 us -> 141 us
  blocking collectives: 117 us -> 0 us
  matrix products: 71.4 us -> 0 us
  local copies, waits for them, and re-layouts: 34.7 us -> 4.35 us
    unnamed x2 -> x0, waiting for transfers between devices: 1260 us -> none
    pallas_call x0 -> x1, Pallas kernels: none -> 141 us  [on_device(): pl.pallas_call(kernel, out_shape=(jax.ShapeDtypeStruct((SEG, QW), BF16),...]
    all_to_all x2 -> x0, blocking collectives: 117 us -> none  [the longest x1 99.8 us: on_device(): lax.all_to_all(send_keys, 'mem', split_axis=0, concat_axis=0, tiled=True)]
    all_to_all x1 -> x0, waiting for transfers between devices: 76.1 us -> none  [on_device(): lax.all_to_all(send_values, 'mem', split_axis=0, concat_axis=0, tiled=True)]
    dot_general x6 -> x0, matrix products: 58.5 us -> none  [the longest x1 23.2 us: on_device(): jnp.einsum('krst,tkd->skrd', d_scores, keys, preferred_element_type=jnp.f...]
  transfers between devices with their start and end apart: 2 -> 0, of which waited for: 2 -> 0; matrix products, arithmetic and copies ran while one was open for 2% -> 0% of each run, Pallas kernels for 0% -> 0%
where the time goes in v1:
time: 146 us
  Pallas kernels  141 us (97%)
  local copies, waits for them, and re-layouts  4.35 us (3%)
    pallas_call x1, Pallas kernels, on_device(): pl.pallas_call(kernel, out_shape=(jax.ShapeDtypeStruct((SEG, QW), BF16),...  141 us
    unnamed x7, local copies, waits for them, and re-layouts  4.35 us

profile of v1, /device:TPU:1, one launch (start us, length us, event | category | flops | bytes accessed | tf_op | source)
XLA Modules:
  0.0 146.0 jit_solution(16671097562928154116)
XLA Ops:
  0.6 141.0 %shard_map.85 = (bf16[512,1024]{1,0:T(8,128)(2,1)}, bf16[512,2048]{1,0:T(8,128)(2,1)}, f32[8,1024]{1,0:T(8,128)}) custom-call(bf16[512,2048]{1,0:T(8,128)(2,1)} %tok_hbm.1, bf16[2048,1024]{1,0:T(8,128)(2,1)} %qw_hbm.1, bf16[1,4,128,512]{3,2,1,0:T(8,128)(2,1)} %mk_hbm.1, bf16[1,4,128,512]{3,2,1,0:T(8,128)(2,1)} %mv_hbm.1, s32[1,1,8]{2,1,0:T(1,128)} %idx.1, ...), custom_call_target="tpu_custom_call" | custom-call | tf_op jit(solution)/shard_map/pallas_call | solution.py:351
  141.6 0.0 copy-start
  141.6 2.4 %copy.12 = bf16[512,1024]{1,0:T(8,128)(2,1)} copy(bf16[512,1024]{1,0:T(8,128)(2,1)} %get-tuple-element.6) | data formatting | bytes 2097152
  144.1 0.0 copy-done
  144.1 0.0 copy-start.1
  144.1 1.3 copy.13
  145.4 0.0 copy-done.1
  145.4 0.6 copy.14
Async XLA Ops:
  141.6 2.4 %copy-start = (bf16[512,2048]{1,0:T(8,128)(2,1)S(1)}, bf16[512,2048]{1,0:T(8,128)(2,1)}, u32[]{:S(2)}) copy-start(bf16[512,2048]{1,0:T(8,128)(2,1)} %get-tuple-element.7) | copy-start | bytes 6291460
  144.1 1.3 copy-start.1

commit v2 on v1

--- a/solution.py
+++ b/solution.py
@@ -31,13 +31,13 @@
 
 def kernel(
     tok_hbm, qw_hbm, mk_hbm, mv_hbm, idx, dctx_hbm,
-    ctx_hbm, gt_hbm, gw_hbm,
-    kv0, kv1, kv2, kv3, tok, qw, dctx, tok_t, qw_t, q, ctx, dq, gt,
+    ctx, gt, gw,
+    kv0, kv1, kv2, kv3, tok, qw, dctx, tok_t, qw_t, q, dq,
     k_sel, k_t, v_one, v_t,
     g_keep, g_send, g_recv, g_sum, dp_recv,
-    za_send, za_recv, zb_send, zb_recv, gw,
+    za_send, za_recv, zb_send, zb_recv,
     in_sem, own_sem, ring_send, ring_recv, sib_send, sib_recv,
-    pair_send, pair_recv, dp_send, dp_rsem, z_send, z_rsem, out_sem,
+    pair_send, pair_recv, dp_send, dp_rsem, z_send, z_rsem,
 ):
     kv = (kv0, kv1, kv2, kv3)
     dp = lax.axis_index("dp")
@@ -129,14 +129,13 @@
                 ring(h, t, way, 1).start()
         to_sib(h, mem)
 
-    def ring_step(h, t, step):
-        for way in range(2):
-            if step < 4 or t == way:
-                ring_arrival(h, t, way, step)
-                if step < 3 or (step == 3 and t == way):
-                    ring(h, t, way, step + 1).start()
-
-    def pass_to_sib(h, step):
+    def ring_step(h, step):
+        for t in range(2):
+            for way in range(2):
+                if step < 4 or t == way:
+                    ring_arrival(h, t, way, step)
+                    if step < 3 or (step == 3 and t == way):
+                        ring(h, t, way, step + 1).start()
         to_sib(h, at_z(-step))
         if step < 4:
             to_sib(h, at_z(step))
@@ -170,17 +169,22 @@
         ds = (e * (d_p - delta)).astype(BF16)
         dq[h, rows, sub] = (dot(ds, k_sel[...]) * (inv * SCALE)).astype(BF16)
 
-    def weight_grad(h):
+    def weight_grad(h, first):
+        j = 1 - core if first else core
+        sub = pl.ds(pl.multiple_of(j * HD, HD), HD)
+
         def tile(i, carry):
-            rows = pl.ds(pl.multiple_of(i * 256, 256), 256)
-            g = dot(tok_t[rows, :], dq[h])
-            lo, hi = g[:, :HD], g[:, HD:]
-            g_keep[rows, :] = jnp.where(core == 0, lo, hi)
-            g_send[h, rows, :] = jnp.where(core == 0, hi, lo).astype(BF16)
+            rows = pl.ds(pl.multiple_of(i * 1024, 1024), 1024)
+            g = dot(tok_t[rows, :], dq[h, :, sub])
+            if first:
+                g_send[h, rows, :] = g.astype(BF16)
+            else:
+                g_keep[rows, :] = g
             return carry
 
-        lax.fori_loop(0, D // 256, tile, 0)
-        pair(h).start()
+        lax.fori_loop(0, D // 1024, tile, 0)
+        if first:
+            pair(h).start()
 
     def pair(h):
         return pltpu.make_async_remote_copy(
@@ -272,41 +276,70 @@
         tok_t[pl.ds(n * 512, 512), :] = tok[:, pl.ds(n * 512, 512)].T
         qw_t[:, pl.ds(n * 512, 512)] = qw[pl.ds(n * 512, 512), :].T
 
-    for h in range(KVH):
-        for step in range(1, 5):
-            ring_step(h, 0, step)
-            if h == 0:
-                project(step - 1)
-            elif step == 2 and h >= 2:
-                dp_start(h - 2)
-            elif step == 3 and h == 1:
-                pass
-            ring_step(h, 1, step)
-            pass_to_sib(h, step)
-            if step == 2 and 1 <= h < KVH - 1:
-                send_own(h + 1)
-            if h == 0:
-                transposes(step - 1)
-                if step == 4:
-                    loads[2].wait()
-            else:
-                attend(h - 1, step <= 2, (step - 1) % 2)
-        if h >= 2:
-            dp_finish(h - 2)
+    def prepare(h):
         sib_all(h).wait_recv()
-        if h >= 1:
-            weight_grad(h - 1)
         gather(h)
 
+    def part(h, n):
+        attend(h, n < 2, n % 2)
+        if n % 2 == 1:
+            weight_grad(h, n < 2)
+
+    ring_step(0, 1)
+    project(0)
+    project(1)
+    ring_step(0, 2)
+    project(2)
+    ring_step(1, 1)
+    project(3)
+    transposes(0)
+    ring_step(0, 3)
+    transposes(1)
+    send_own(2)
+    ring_step(0, 4)
+    transposes(2)
+    ring_step(1, 2)
+    transposes(3)
+    loads[2].wait()
+    prepare(0)
+    part(0, 0)
+    ring_step(2, 1)
+    part(0, 1)
+    ring_step(1, 3)
+    part(0, 2)
+    send_own(3)
+    ring_step(1, 4)
+    part(0, 3)
+    ring_step(2, 2)
+    prepare(1)
+    part(1, 0)
+    dp_start(0)
+    ring_step(3, 1)
+    part(1, 1)
+    ring_step(2, 3)
+    part(1, 2)
+    ring_step(2, 4)
+    part(1, 3)
+    ring_step(3, 2)
+    prepare(2)
+    part(2, 0)
+    dp_start(1)
+    ring_step(3, 3)
+    part(2, 1)
+    part(2, 2)
+    part(2, 3)
+    dp_finish(0)
+    ring_step(3, 4)
     dp_start(2)
-    for step in range(4):
-        attend(3, step < 2, step % 2)
-    weight_grad(3)
+    prepare(3)
+    part(3, 0)
+    part(3, 1)
+    part(3, 2)
+    part(3, 3)
+    dp_start(3)
+    dp_finish(1)
     dp_finish(2)
     z_start(0, za_send, za_recv)
-    ctx_out = pltpu.make_async_copy(ctx, ctx_hbm, out_sem.at[0])
-    ctx_out.start()
-    dp_start(3)
 
     def tokens_tile(n, carry):
         cols = pl.ds(pl.multiple_of(n * 512, 512), 512)
@@ -317,14 +350,10 @@
         return carry
 
     lax.fori_loop(0, D // 512, tokens_tile, 0)
-    gt_out = pltpu.make_async_copy(gt, gt_hbm, out_sem.at[1])
-    gt_out.start()
     z_finish(0, za_send, za_recv, (0, 1, 2))
     dp_finish(3)
     z_start(1, zb_send, zb_recv)
     z_finish(1, zb_send, zb_recv, (3,))
-    gw_out = pltpu.make_async_copy(gw, gw_hbm, out_sem.at[2])
-    gw_out.start()
 
     for h in range(KVH):
         for t in range(2):
@@ -338,9 +367,6 @@
         dp_all(h).wait_send()
     z_all(0, za_recv).wait_send()
     z_all(1, zb_recv).wait_send()
-    ctx_out.wait()
-    gt_out.wait()
-    gw_out.wait()
 
 
 def on_device(tokens, q_weight, memory_keys, memory_values, retrieved_block_index, d_context):
@@ -351,12 +377,12 @@
     return pl.pallas_call(
         kernel,
         out_shape=(
-            jax.ShapeDtypeStruct((SEG, QW), BF16),
-            jax.ShapeDtypeStruct((SEG, D), BF16),
-            jax.ShapeDtypeStruct((D // (NDP * NMEM), QW), F32),
+            vmem((SEG, QW), BF16),
+            vmem((SEG, D), BF16),
+            vmem((D // (NDP * NMEM), QW), F32),
         ),
         in_specs=[hbm, hbm, hbm, hbm, pl.BlockSpec(memory_space=pltpu.SMEM), hbm],
-        out_specs=(hbm, hbm, hbm),
+        out_specs=(pl.BlockSpec(memory_space=vmem),) * 3,
         scratch_shapes=[
             kv, kv, kv, kv,
             vmem((SEG, D), BF16),
@@ -365,9 +391,7 @@
             vmem((D, SEG), BF16),
             vmem((QW, D), BF16),
             vmem((KVH, SEG, 256), BF16),
-            vmem((SEG, QW), BF16),
             vmem((KVH, SEG, 256), BF16),
-            vmem((SEG, D), BF16),
             vmem((TOPB * 128, HD), BF16),
             vmem((HD, TOPB * 128), BF16),
             vmem((TOPB * 128, 2 * HD), BF16),
@@ -381,7 +405,6 @@
             vmem((NMEM - 1, 8, 3 * HD), F32),
             vmem((NMEM, 8, HD), F32),
             vmem((NMEM - 1, 8, HD), F32),
-            vmem((8, QW), F32),
             dma((3,)),
             dma((KVH, 2)),
             dma((KVH, 2)),
@@ -394,10 +417,9 @@
             dma((KVH,)),
             dma((2,)),
             dma((2,)),
-            dma((3,)),
         ],
         compiler_params=pltpu.CompilerParams(
-            collective_id=0, has_side_effects=True, vmem_limit_bytes=60 * 1024 * 1024
+            collective_id=0, has_side_effects=True, vmem_limit_bytes=52 * 1024 * 1024
         ),
     )(tokens, q_weight, memory_keys, memory_values, retrieved_block_index, d_context)
 

time: 146 us -> 125 us (0.86)
  Pallas kernels: 141 us -> 121 us
    pallas_call x1, Pallas kernels: 141 us -> 121 us  [on_device(): pl.pallas_call(kernel, out_shape=(vmem((SEG, QW), BF16), vmem((SEG, D), B...]
    unnamed x7 -> x3, local copies, waits for them, and re-layouts: 4.35 us -> 2.91 us
where the time goes in v2:
time: 125 us
  Pallas kernels  121 us (97%)
  local copies, waits for them, and re-layouts  2.91 us (2%)
    pallas_call x1, Pallas kernels, on_device(): pl.pallas_call(kernel, out_shape=(vmem((SEG, QW), BF16), vmem((SEG, D), B...  121 us
    unnamed x3, local copies, waits for them, and re-layouts  2.91 us

profile of v2, /device:TPU:1, one launch (start us, length us, event | category | flops | bytes accessed | tf_op | source)
XLA Modules:
  0.0 124.9 jit_solution(18023989040565875647)
XLA Ops:
  0.6 121.3 %shard_map.85 = (bf16[512,1024]{1,0:T(8,128)(2,1)S(1)}, bf16[512,2048]{1,0:T(8,128)(2,1)S(1)}, f32[8,1024]{1,0:T(8,128)S(1)}) custom-call(bf16[512,2048]{1,0:T(8,128)(2,1)} %tok_hbm.1, bf16[2048,1024]{1,0:T(8,128)(2,1)} %qw_hbm.1, bf16[1,4,128,512]{3,2,1,0:T(8,128)(2,1)} %mk_hbm.1, bf16[1,4,128,512]{3,2,1,0:T(8,128)(2,1)} %mv_hbm.1, s32[1,1,8]{2,1,0:T(1,128)} %idx.1, ...), custom_call_target="tpu_custom_call" | custom-call | tf_op jit(solution)/shard_map/pallas_call | solution.py:377
  122.0 1.0 copy.12
  122.9 0.6 copy.14
  123.5 1.3 %copy.13 = bf16[512,2048]{1,0:T(8,128)(2,1)} copy(bf16[512,2048]{1,0:T(8,128)(2,1)S(1)} %get-tuple-element.4) | data formatting | bytes 4194304
